TPU v7x, 128 devices: a whole 4x4x4 slice. The times are simulated.
128 devices in a mesh: clus: 4 (over x), split: 32 (over z, y, core).
Axes of the slice: x: 4, y: 4, z: 4, core: 2. Of those that a mesh axis runs over, the one named last changes fastest.
Arguments:
- embeddings: float32 [16384, 4096], P(('clus', 'split'))
- cluster_ids: int32 [16384], P(('clus', 'split')), may hold values from 0 to 63, as said below
Outputs:
- best_similarity: float32 [16384], P(('clus', 'split'))
Inputs may be any that keep to these rules, and one draw needn't show every extreme that they name: `cluster_ids`: the documents of one device's shard hold at most 64 cluster ids with any one residue modulo 4, and every shard has a residue reached exactly 64 times. Some clusters hold a single document.
All inputs are finite; a program needn't handle non-finite values.
Results may differ from a plain program's by a relative error of at most 0.0003.
Values may be sent and summed in bfloat16 or wider, within the bound.
No kernel may reach another device: no remote copies, remote signals or barrier semaphores. Data moves between devices by JAX's collectives and lax.ppermute only.
A program may use at most 192 MiB of HBM per device.

v0:
```python
import jax
import jax.numpy as jnp
from jax import lax
from jax.sharding import PartitionSpec as P


def masked_scores(left, left_ids, right, right_ids, left_start):
    scores = lax.dot_general(
        left, right, (((1,), (1,)), ((), ())), preferred_element_type=jnp.float32
    )
    left_at = left_start + jnp.arange(left.shape[0], dtype=jnp.int32)
    right_at = jnp.arange(right.shape[0], dtype=jnp.int32)
    mask = (
        (left_ids[:, None] == right_ids[None, :])
        & (left_ids[:, None] >= 0)
        & (left_at[:, None] != right_at[None, :])
    )
    return jnp.where(mask, scores, -1.0)


def normalise_rows(values):
    squares = jnp.sum(values * values, axis=1, keepdims=True)
    return (values * lax.rsqrt(squares + 1e-06)).astype(jnp.bfloat16)


def on_device(embeddings, cluster_ids):
    rows = embeddings.shape[0]
    groups = lax.axis_size("clus")
    cap = 2 * rows // groups
    slots = groups * cap
    owner_of = cluster_ids % groups
    onehot = (owner_of[:, None] == jnp.arange(groups, dtype=jnp.int32)[None, :]).astype(jnp.int32)
    before = jnp.cumsum(onehot, axis=0) - onehot
    rank = jnp.sum(before * onehot, axis=1)
    place = owner_of * cap + rank
    picked = place[None, :] == jnp.arange(slots, dtype=jnp.int32)[:, None]
    filled = jnp.any(picked, axis=1)
    source = jnp.sum(jnp.where(picked, jnp.arange(rows, dtype=jnp.int32)[None, :], 0), axis=1)
    out_labels = jnp.where(filled, cluster_ids[source], -1)
    local_unit = normalise_rows(embeddings)
    outgoing_unit = jnp.where(filled[:, None], local_unit[source], jnp.zeros((), jnp.bfloat16))
    unit, labels = (
        lax.all_to_all(outgoing_unit, "clus", split_axis=0, concat_axis=0, tiled=True),
        lax.all_to_all(out_labels, "clus", split_axis=0, concat_axis=0, tiled=True),
    )
    own_start = lax.axis_index("split") * slots
    floor_values = jnp.full((slots,), -1.0, jnp.float32)
    scores = masked_scores(
        unit,
        labels,
        lax.all_gather(unit, "split", axis=0, tiled=True),
        lax.all_gather(labels, "split", axis=0, tiled=True),
        own_start,
    )
    best = jnp.maximum(floor_values, jnp.max(scores, axis=1))
    returned_max = lax.all_to_all(best, "clus", split_axis=0, concat_axis=0, tiled=True)
    return returned_max[place]


def solution(mesh):
    in_specs = (P(("clus", "split"), None), P(("clus", "split")))
    out_specs = P(("clus", "split"))
    return jax.shard_map(
        on_device, mesh=mesh, in_specs=in_specs, out_specs=out_specs, check_vma=False
    )
```

profile of v0, /device:TPU:0, one launch (start us, length us, event | category | flops | bytes accessed | tf_op | source)
XLA Modules:
  0.0 294.9 jit_solution(16780526485380917887)
XLA Ops:
  6.5 0.8 and_select_fusion
  7.4 0.1 fusion.3
  7.4 0.2 reduce_window_sum.11
  7.6 0.2 select_reduce_fusion.1
  7.8 0.7 compare_select_fusion.1
  8.5 0.1 select_reduce_fusion
  8.6 0.1 fusion.2
  8.7 1.8 multiply_reduce_fusion
  10.6 0.2 multiply_convert_fusion
  10.8 0.1 broadcast_in_dim.57
  10.9 1.8 gather_fusion.1
  12.7 0.2 broadcast_select_fusion
  12.9 30.6 %all_to_all.24 = bf16[4,64,4096]{2,1,0:T(8,128)(2,1)} all-to-all(bf16[4,64,4096]{2,1,0:T(8,128)(2,1)S(1)} %broadcast_select_fusion), channel_id=1, replica_groups=mesh['clus'=4,'split'=32] {'clus'}, dimensions={0} | all-to-all | bytes 4194304 | tf_op jit(solution)/shard_map/all_to_all | solution.py:43
  43.6 0.6 copy-done
  44.2 1.9 gather_fusion
  46.1 0.7 select_n.52
  46.8 3.2 %all-to-all-start = ((s32[4,64,1]{1,2,0:T(1,128)}), s32[4,64,1]{1,2,0:T(1,128)S(1)}, u32[]{:S(2)}, u32[]{:S(2)}) async-start(s32[4,64,1]{1,2,0:T(1,128)} %bitcast.2), calls=%async_computation | async-start | bytes 4096 | tf_op jit(solution)/shard_map/all_to_all | solution.py:44
  50.0 5.1 %all-to-all-done = s32[4,64,1]{1,2,0:T(1,128)S(1)} async-done(((s32[4,64,1]{1,2,0:T(1,128)}), s32[4,64,1]{1,2,0:T(1,128)S(1)}, u32[]{:S(2)}, u32[]{:S(2)}) %all-to-all-start) | async-done | bytes 1056 | tf_op jit(solution)/shard_map/all_to_all | solution.py:44
  55.1 0.5 broadcast.98
  55.6 0.7 reduce.8
  56.2 0.1 eq.49
  56.3 0.1 reshape.103
  56.4 25.7 %all-gather = s32[32,1,256]{2,1,0:T(1,128)S(1)} all-gather(s32[1,1,256]{2,1,0:T(1,128)S(1)} %reshape.103), channel_id=1, replica_groups=mesh['clus'=4,'split'=32] {'split'}, dimensions={0}, use_global_device_ids=true | all-gather | bytes 33792 | tf_op jit(solution)/shard_map/all_gather | solution.py:52
  82.1 163.5 %all-gather.3.cloned.1.call-done = bf16[8192,4096]{1,0:T(8,128)(2,1)} async-done(((bf16[256,4096]{1,0:T(8,128)(2,1)}), bf16[8192,4096]{1,0:T(8,128)(2,1)}) %all-gather.3.cloned.1.call-update) | async-done | bytes 67108880 | tf_op jit(solution)/shard_map/all_gather | solution.py:51
  245.6 29.4 %fusion.1 = f32[256]{0:T(256)S(1)} fusion(bf16[256,4096]{1,0:T(8,128)(2,1)S(1)} %bitcast.14, bf16[8192,4096]{1,0:T(8,128)(2,1)} %all-gather.3.cloned.1.call-done, s32[256]{0:T(256)S(1)} %iota_add_fusion, pred[256]{0:T(512)(128)(4,1)S(1)} %broadcast_compare_fusion, s32[8192]{0:T(1024)S(1)} %bitcast.15, s32[256]{0:T(256)S(1)} %eq.49), kind=kOutput, calls=%fused_computation.9 | convolution fusion | flops 17192452096 | bytes 69242112 | tf_op jit(solution)/shard_map/dot_general | solution.py:8
  275.0 0.7 max_broadcast_in_dim.14
  275.6 4.2 %all-to-all-start.2 = ((f32[4,64,1]{1,2,0:T(1,128)}), f32[4,64,1]{1,2,0:T(1,128)S(1)}, u32[]{:S(2)}, u32[]{:S(2)}) async-start(f32[4,64,1]{1,2,0:T(1,128)} %bitcast.6), calls=%async_computation.2 | async-start | bytes 4096 | tf_op jit(solution)/shard_map/all_to_all | solution.py:56
  279.9 5.1 %all-to-all-done.2 = f32[4,64,1]{1,2,0:T(1,128)S(1)} async-done(((f32[4,64,1]{1,2,0:T(1,128)}), f32[4,64,1]{1,2,0:T(1,128)S(1)}, u32[]{:S(2)}, u32[]{:S(2)}) %all-to-all-start.2) | async-done | bytes 1056 | tf_op jit(solution)/shard_map/all_to_all | solution.py:56
  285.0 0.5 broadcast.99
  285.5 0.7 reduce.9
  286.2 0.1 all_to_all.20
  286.3 1.8 gather_fusion.2
  (15 shorter events, 0.1 us)
Async XLA Ops:
  6.5 4.0 %copy-start.1 = (f32[128,4096]{1,0:T(8,128)S(1)}, f32[128,4096]{1,0:T(8,128)}, u32[]{:S(2)}) copy-start(f32[128,4096]{1,0:T(8,128)} %param.2) | copy-start | bytes 6291460
  6.5 239.0 %all-gather.3.cloned.1.call-start = ((), (), s32[]{:S(2)}) async-start(), calls=%async_computation.3 | async-start | bytes 69206016 | tf_op jit(solution)/shard_map/all_gather | solution.py:51
  43.5 0.7 copy-start
  43.6 202.0 %copy-start.2 = (bf16[4,64,4096]{2,1,0:T(8,128)(2,1)S(1)}, bf16[4,64,4096]{2,1,0:T(8,128)(2,1)}, u32[]{:S(2)}) copy-start(bf16[4,64,4096]{2,1,0:T(8,128)(2,1)} %all_to_all.24) | copy-start | bytes 6291460
  46.8 8.3 %all-to-all-start = ((s32[4,64,1]{1,2,0:T(1,128)}), s32[4,64,1]{1,2,0:T(1,128)S(1)}, u32[]{:S(2)}, u32[]{:S(2)}) async-start(s32[4,64,1]{1,2,0:T(1,128)} %bitcast.2), calls=%async_computation | async-start | bytes 4096 | tf_op jit(solution)/shard_map/all_to_all | solution.py:44
  275.6 9.4 %all-to-all-start.2 = ((f32[4,64,1]{1,2,0:T(1,128)}), f32[4,64,1]{1,2,0:T(1,128)S(1)}, u32[]{:S(2)}, u32[]{:S(2)}) async-start(f32[4,64,1]{1,2,0:T(1,128)} %bitcast.6), calls=%async_computation.2 | async-start | bytes 4096 | tf_op jit(solution)/shard_map/all_to_all | solution.py:56
Sparse Core Ops, SparseCore 0:
  43.7 201.8 all-gather.2
where the time goes:
time: 295 us
  waiting for transfers between devices  174 us (59%)
  blocking collectives  56.3 us (19%)
  matrix products  29.4 us (10%)
  between operations  13.5 us (5%)
  local copies, waits for them, and re-layouts  8.82 us (3%)
  starting transfers between devices  7.47 us (3%)
  other arithmetic  5.76 us (2%)
    all_gather x1, waiting for transfers between devices, on_device(): lax.all_gather(unit, 'split', axis=0, tiled=True)  164 us
    all_to_all x1, blocking collectives, on_device(): lax.all_to_all(outgoing_unit, 'clus', split_axis=0, concat_axis=0, tiled=...  30.6 us
    dot_general x1, matrix products, masked_scores(): lax.dot_general(left, right, (((1,), (1,)), ((), ())), preferred_element_...  29.4 us
    all_gather x1, blocking collectives, on_device(): lax.all_gather(labels, 'split', axis=0, tiled=True)  25.7 us
  transfers between devices with their start and end apart: 3, of which 3 were waited for; matrix products, arithmetic and copies ran while one was open for 1% of the time, Pallas kernels for 0%

commit v1 on v0

--- a/solution.py
+++ b/solution.py
@@ -48,7 +48,9 @@
     scores = masked_scores(
         unit,
         labels,
-        lax.all_gather(unit, "split", axis=0, tiled=True),
+        jnp.concatenate(
+            lax.all_to_all(jnp.stack([unit] * lax.axis_size("split")), "split", 0, 0), axis=0
+        ),
         lax.all_gather(labels, "split", axis=0, tiled=True),
         own_start,
     )

time: 295 us -> 990 us (3.36)
  blocking collectives: 56.3 us -> 901 us
  waiting for transfers between devices: 174 us -> 5.06 us
  local copies, waits for them, and re-layouts: 8.82 us -> 29.3 us
  between operations: 13.5 us -> 0.1 us
    all_gather x1, blocking collectives: 25.7 us -> 870 us  [on_device(): lax.all_gather(labels, 'split', axis=0, tiled=True)]
    all_gather x1 -> x0, waiting for transfers between devices: 164 us -> none  [on_device(): lax.all_gather(unit, 'split', axis=0, tiled=True)]
    another operation x0 -> x1, local copies, waits for them, and re-layouts: none -> 21 us  [on_device(): jnp.stack([unit] * lax.axis_size('split'))]
  transfers between devices with their start and end apart: 3 -> 3, of which waited for: 3 -> 1; matrix products, arithmetic and copies ran while one was open for 1% -> 1% of each run, Pallas kernels for 0% -> 0%
where the time goes in v1:
time: 990 us; the launch traced here: 988 us
  blocking collectives  901 us (91%)
  local copies, waits for them, and re-layouts  29.3 us (3%)
  matrix products  29.3 us (3%)
  starting transfers between devices  16.1 us (2%)
    all_gather x1, blocking collectives, on_device(): lax.all_gather(labels, 'split', axis=0, tiled=True)  870 us
    all_to_all x1, blocking collectives, on_device(): lax.all_to_all(outgoing_unit, 'clus', split_axis=0, concat_axis=0, tiled=...  30.6 us
    dot_general x1, matrix products, masked_scores(): lax.dot_general(left, right, (((1,), (1,)), ((), ())), preferred_element_...  29.3 us
    another operation x1, local copies, waits for them, and re-layouts, on_device(): jnp.stack([unit] * lax.axis_size('split'))  21 us
  transfers between devices with their start and end apart: 3, of which 1 were waited for; matrix products, arithmetic and copies ran while one was open for 1% of the time, Pallas kernels for 0%

profile of v1, /device:TPU:0, one launch (start us, length us, event | category | flops | bytes accessed | tf_op | source)
XLA Modules:
  0.0 987.7 jit_solution(2911523991870402585)
XLA Ops:
  0.0 0.8 and_select_fusion
  0.8 0.1 fusion.3
  0.9 0.2 reduce_window_sum.11
  1.1 0.2 select_reduce_fusion.1
  1.3 0.7 compare_select_fusion.1
  1.9 0.1 select_reduce_fusion
  2.0 0.1 fusion.2
  2.2 1.9 gather_fusion
  4.1 0.7 select_n.52
  4.8 4.4 all-to-all-start
  9.2 0.1 broadcast_in_dim.57
  9.2 1.8 multiply_reduce_fusion
  11.1 0.2 multiply_convert_fusion
  11.3 1.8 gather_fusion.1
  13.2 1.6 broadcast_select_fusion
  14.7 0.0 all-to-all-done
  14.7 30.6 %all_to_all.29 = bf16[4,64,4096]{2,1,0:T(8,128)(2,1)S(1)} all-to-all(bf16[4,64,4096]{2,1,0:T(8,128)(2,1)} %broadcast_select_fusion), channel_id=1, replica_groups=mesh['clus'=4,'split'=32] {'clus'}, dimensions={0} | all-to-all | bytes 4194304 | tf_op jit(solution)/shard_map/all_to_all | solution.py:43
  45.3 21.0 %stack.2 = bf16[32,256,4096]{2,1,0:T(8,128)(2,1)} broadcast(bf16[256,4096]{1,0:T(8,128)(2,1)S(1)} %bitcast.13), dimensions={1,2} | broadcast | bytes 69206016 | tf_op jit(solution)/shard_map/stack | solution.py:52
  66.3 8.5 all-to-all-start.2
  74.8 0.5 broadcast.99
  75.3 0.7 reduce.8
  76.0 0.1 eq.49
  76.1 0.1 reshape.110
  76.2 870.2 %all-gather = s32[32,1,256]{2,1,0:T(1,128)S(1)} all-gather(s32[1,1,256]{2,1,0:T(1,128)S(1)} %reshape.110), channel_id=1, replica_groups=mesh['clus'=4,'split'=32] {'split'}, dimensions={0}, use_global_device_ids=true | all-gather | bytes 33792 | tf_op jit(solution)/shard_map/all_gather | solution.py:54
  946.3 29.3 %fusion.1 = f32[256]{0:T(256)S(1)} fusion(bf16[256,4096]{1,0:T(8,128)(2,1)S(1)} %bitcast.14, bf16[8192,4096]{1,0:T(8,128)(2,1)} %bitcast.6, s32[256]{0:T(256)S(1)} %iota_add_fusion, pred[256]{0:T(512)(128)(4,1)S(1)} %broadcast_compare_fusion, s32[8192]{0:T(1024)S(1)} %bitcast.16, s32[256]{0:T(256)S(1)} %eq.49), kind=kOutput, calls=%fused_computation.9 | convolution fusion | flops 17192452096 | bytes 69242112 | tf_op jit(solution)/shard_map/dot_general | solution.py:8
  975.7 0.7 max_broadcast_in_dim.14
  976.3 3.2 all-to-all-start.3
  979.6 5.1 all-to-all-done.3
  984.7 0.5 broadcast.100
  985.2 0.7 reduce.9
  985.8 0.1 all_to_all.24
  985.9 1.8 gather_fusion.2
  (11 shorter events, 0.1 us)
Async XLA Ops:
  0.0 11.1 %copy-start = (f32[128,4096]{1,0:T(8,128)S(1)}, f32[128,4096]{1,0:T(8,128)}, u32[]{:S(2)}) copy-start(f32[128,4096]{1,0:T(8,128)} %param.2) | copy-start | bytes 6291460
  4.8 9.9 %all-to-all-start = ((s32[4,64,1]{1,2,0:T(1,128)}), s32[4,64,1]{1,2,0:T(1,128)S(1)}, u32[]{:S(2)}, u32[]{:S(2)}) async-start(s32[4,64,1]{1,2,0:T(1,128)} %bitcast.2), calls=%async_computation | async-start | bytes 4096 | tf_op jit(solution)/shard_map/all_to_all | solution.py:44
  66.3 880.0 %all-to-all-start.2 = ((bf16[32,256,4096]{2,1,0:T(8,128)(2,1)}), bf16[32,256,4096]{2,1,0:T(8,128)(2,1)}, u32[]{:S(2)}, u32[]{:S(2)}) async-start(bf16[32,256,4096]{2,1,0:T(8,128)(2,1)} %stack.2), calls=%async_computation.2 | async-start | bytes 134217728 | tf_op jit(solution)/shard_map/all_to_all | solution.py:52
  976.3 8.3 all-to-all-start.3
